TPU v7x, 32 devices: a whole 2x2x4 slice. The times are simulated.
32 devices in a mesh: row: 2 (over y), col: 4 (over z), vc: 4 (over x, core).
Axes of the slice: x: 2, y: 2, z: 4, core: 2. Of those that a mesh axis runs over, the one named last changes fastest.
Arguments:
- amplitudes: bfloat16 [8, 8, 128, 128], P('row', 'col'), may hold values from -6 to 6
- factors: bfloat16 [2, 4, 256, 128, 128], P('row', 'col', 'vc'), may hold values from -0.125 to 0.125
- pno_counts: int32 [8, 8], P('row', 'col'), may hold values from 32 to 128, as said below
- pair_live: int32 [8, 8], P('row', 'col'), may hold values from 0 to 1, as said below
Outputs:
- residual_ladder: float32 [8, 8, 128, 128], P('row', 'col', 'vc')
Inputs may be any that keep to these rules, and one draw needn't show every extreme that they name: pno_counts[i, j] equals pno_counts[j, i]; every diagonal entry is 128. pair_live[i, j] equals pair_live[j, i]; every diagonal entry is 1.
All inputs are finite; a program needn't handle non-finite values.
Results may differ from a plain program's by a relative error of at most 0.0028.
Values sent between devices are 32-bit elements; how exact they have to be, the bound alone decides.
No kernel may reach another device: no remote copies, remote signals or barrier semaphores. Data moves between devices by JAX's collectives and lax.ppermute only.
A program may use at most 64 MiB of HBM per device.

v0:
```python
import jax
import jax.numpy as jnp
from jax import lax
from jax.sharding import PartitionSpec as P


def ladder_tile(domain, masked):
    half_tile = jnp.einsum(
        "qac,cd->qad", domain, masked, preferred_element_type=jnp.float32
    ).astype(jnp.bfloat16)
    return jnp.einsum("qad,qbd->ab", half_tile, domain, preferred_element_type=jnp.float32)


def mirrored_pairs(payload):
    row_slots, col_slots, height, breadth = payload.shape
    sectioned = payload.reshape(2, row_slots // 2, col_slots, height, breadth)
    arrived = lax.all_to_all(
        lax.all_to_all(sectioned, "row", split_axis=3, concat_axis=0, tiled=True),
        "col",
        split_axis=0,
        concat_axis=0,
        tiled=True,
    )
    arrived = lax.all_to_all(arrived, "row", split_axis=0, concat_axis=3, tiled=True)
    return jnp.transpose(arrived, (0, 2, 1, 3, 4)).reshape(row_slots, col_slots, height, breadth)


def on_device(amplitudes, factors, pno_counts, pair_live):
    row_slots, col_slots, virtuals = (amplitudes.shape[0], amplitudes.shape[1], amplitudes.shape[2])
    domain = factors[0, 0]
    positions = lax.broadcasted_iota(jnp.int32, (virtuals,), 0)
    pair_tiles = []
    for row_slot in range(row_slots):
        for col_slot in range(col_slots):
            inside = (positions < pno_counts[row_slot, col_slot]).astype(jnp.bfloat16)
            masked = amplitudes[row_slot, col_slot] * inside[:, None] * inside[None, :]
            ladder_term = ladder_tile(domain, masked)
            pair_tiles.append(ladder_term)
    partials = jnp.stack(pair_tiles).reshape(row_slots, col_slots, virtuals, virtuals)
    slab_rows = virtuals // lax.axis_size("vc")
    vc_index = lax.axis_index("vc")
    ladder_sum = lax.psum(partials, "vc")
    own_rows = lax.dynamic_slice_in_dim(ladder_sum, vc_index * slab_rows, slab_rows, 2)
    flipped = jnp.swapaxes(
        lax.dynamic_slice_in_dim(ladder_sum, vc_index * slab_rows, slab_rows, 3), 2, 3
    )
    summed = own_rows + mirrored_pairs(flipped)
    rows_here = vc_index * slab_rows + lax.broadcasted_iota(jnp.int32, (slab_rows,), 0)
    inside_rows = rows_here[None, None, :] < pno_counts[:, :, None]
    inside_cols = positions[None, None, :] < pno_counts[:, :, None]
    kept_cells = (
        inside_rows[:, :, :, None] & inside_cols[:, :, None, :] & (pair_live[:, :, None, None] > 0)
    )
    return jnp.where(kept_cells, summed, jnp.zeros_like(summed))


def solution(mesh):
    in_specs = (
        P("row", "col", None, None),
        P("row", "col", "vc", None, None),
        P("row", "col"),
        P("row", "col"),
    )
    out_specs = P("row", "col", "vc", None)
    return jax.shard_map(
        on_device, mesh=mesh, in_specs=in_specs, out_specs=out_specs, check_vma=False
    )
```

profile of v0, /device:TPU:0, one launch (start us, length us, event | category | flops | bytes accessed | tf_op | source)
XLA Modules:
  0.0 103.0 jit_solution(980079473971213598)
XLA Ops:
  6.5 0.0 copy-start
  6.5 0.0 all-reduce.2.cloned.1.call-start
  6.5 1.7 %fusion.289 = (s32[1,1]{0,1:T(1,128)}, s32[1,1]{0,1:T(1,128)}, s32[1,1]{0,1:T(1,128)}, s32[1,1]{0,1:T(1,128)}, s32[1,1]{0,1:T(1,128)}, /*index=5*/s32[1,1]{0,1:T(1,128)}, s32[1,1]{0,1:T(1,128)}, s32[1,1]{0,1:T(1,128)}) fusion(s32[4,2]{0,1:T(2,128)} %param.6), kind=kLoop, calls=%fused_computation.127 | loop fusion | bytes 64 | tf_op jit(solution)/shard_map/slice | solution.py:35
  8.2 0.6 compare_convert_fusion.7
  8.8 0.6 compare_convert_fusion.6
  9.5 0.6 compare_convert_fusion.5
  10.1 0.6 compare_convert_fusion.4
  10.7 0.6 compare_convert_fusion.3
  11.3 0.5 compare_convert_fusion.2
  11.9 0.7 compare_convert_fusion.1
  12.6 0.7 compare_convert_fusion
  13.2 0.0 copy-done
  13.2 0.0 copy-start.2
  13.3 2.6 %fusion.87 = f32[8,128,128]{2,1,0:T(8,128)S(1)} fusion(bf16[1,1,64,128,128]{4,3,2,1,0:T(8,128)(2,1)S(1)} %copy-done, bf16[4,2,128,128]{3,2,1,0:T(8,128)(2,1)} %param.4, bf16[128]{0:T(256)(128)(2,1)S(1)} %compare_convert_fusion.7), kind=kOutput, calls=%fused_computation.49 | convolution fusion | flops 538017792 | bytes 4293632 | tf_op jit(solution)/shard_map/qad,qbd->ab/dot_general | solution.py:11
  15.9 0.0 copy-done.2
  15.9 1.8 %fusion.101 = f32[8,128,128]{2,1,0:T(8,128)S(1)} fusion(f32[8,128,128]{2,1,0:T(8,128)S(1)} %fusion.87, bf16[1,1,64,128,128]{4,3,2,1,0:T(8,128)(2,1)S(1)} %copy-done, bf16[4,2,128,128]{3,2,1,0:T(8,128)(2,1)S(1)} %copy-done.2, bf16[128]{0:T(256)(128)(2,1)S(1)} %compare_convert_fusion.6), kind=kOutput, calls=%fused_computation.51 | convolution fusion | flops 538017792 | bytes 4293632 | tf_op jit(solution)/shard_map/qad,qbd->ab/dot_general | solution.py:11
  17.7 1.8 %fusion.115 = f32[8,128,128]{2,1,0:T(8,128)S(1)} fusion(f32[8,128,128]{2,1,0:T(8,128)S(1)} %fusion.101, bf16[1,1,64,128,128]{4,3,2,1,0:T(8,128)(2,1)S(1)} %copy-done, bf16[4,2,128,128]{3,2,1,0:T(8,128)(2,1)S(1)} %copy-done.2, bf16[128]{0:T(256)(128)(2,1)S(1)} %compare_convert_fusion.5), kind=kOutput, calls=%fused_computation.53 | convolution fusion | flops 538017792 | bytes 4293632 | tf_op jit(solution)/shard_map/qad,qbd->ab/dot_general | solution.py:11
  19.5 1.8 %fusion.129 = f32[8,128,128]{2,1,0:T(8,128)S(1)} fusion(f32[8,128,128]{2,1,0:T(8,128)S(1)} %fusion.115, bf16[1,1,64,128,128]{4,3,2,1,0:T(8,128)(2,1)S(1)} %copy-done, bf16[4,2,128,128]{3,2,1,0:T(8,128)(2,1)S(1)} %copy-done.2, bf16[128]{0:T(256)(128)(2,1)S(1)} %compare_convert_fusion.4), kind=kOutput, calls=%fused_computation.55 | convolution fusion | flops 538017792 | bytes 4293632 | tf_op jit(solution)/shard_map/qad,qbd->ab/dot_general | solution.py:11
  21.3 1.8 %fusion.143 = f32[8,128,128]{2,1,0:T(8,128)S(1)} fusion(f32[8,128,128]{2,1,0:T(8,128)S(1)} %fusion.129, bf16[1,1,64,128,128]{4,3,2,1,0:T(8,128)(2,1)S(1)} %copy-done, bf16[4,2,128,128]{3,2,1,0:T(8,128)(2,1)S(1)} %copy-done.2, bf16[128]{0:T(256)(128)(2,1)S(1)} %compare_convert_fusion.3), kind=kOutput, calls=%fused_computation.57 | convolution fusion | flops 538017792 | bytes 4293632 | tf_op jit(solution)/shard_map/qad,qbd->ab/dot_general | solution.py:11
  23.1 1.8 %fusion.157 = f32[8,128,128]{2,1,0:T(8,128)S(1)} fusion(f32[8,128,128]{2,1,0:T(8,128)S(1)} %fusion.143, bf16[1,1,64,128,128]{4,3,2,1,0:T(8,128)(2,1)S(1)} %copy-done, bf16[4,2,128,128]{3,2,1,0:T(8,128)(2,1)S(1)} %copy-done.2, bf16[128]{0:T(256)(128)(2,1)S(1)} %compare_convert_fusion.2), kind=kOutput, calls=%fused_computation.59 | convolution fusion | flops 538017792 | bytes 4293632 | tf_op jit(solution)/shard_map/qad,qbd->ab/dot_general | solution.py:11
  24.9 1.8 %fusion.171 = f32[8,128,128]{2,1,0:T(8,128)S(1)} fusion(f32[8,128,128]{2,1,0:T(8,128)S(1)} %fusion.157, bf16[1,1,64,128,128]{4,3,2,1,0:T(8,128)(2,1)S(1)} %copy-done, bf16[4,2,128,128]{3,2,1,0:T(8,128)(2,1)S(1)} %copy-done.2, bf16[128]{0:T(256)(128)(2,1)S(1)} %compare_convert_fusion.1), kind=kOutput, calls=%fused_computation.61 | convolution fusion | flops 538017792 | bytes 4293632 | tf_op jit(solution)/shard_map/qad,qbd->ab/dot_general | solution.py:11
  26.7 0.0 copy-start.3
  26.7 1.8 %fusion.185 = f32[8,128,128]{2,1,0:T(8,128)S(1)} fusion(f32[8,128,128]{2,1,0:T(8,128)S(1)} %fusion.171, bf16[1,1,64,128,128]{4,3,2,1,0:T(8,128)(2,1)S(1)} %copy-done, bf16[4,2,128,128]{3,2,1,0:T(8,128)(2,1)S(1)} %copy-done.2, bf16[128]{0:T(256)(128)(2,1)S(1)} %compare_convert_fusion), kind=kOutput, calls=%fused_computation.63 | convolution fusion | flops 538017792 | bytes 4293632 | tf_op jit(solution)/shard_map/qad,qbd->ab/dot_general | solution.py:11
  28.5 0.0 copy-start.1
  28.5 0.0 copy-start.4
  28.5 0.8 copy-done.1
  29.3 0.0 all-reduce.2.cloned.1.call-update
  29.3 0.0 copy-done.3
  29.3 0.1 copy.58
  29.4 35.9 %all-reduce.2.cloned.1.call-done = f32[4,2,128,128]{3,2,1,0:T(8,128)} async-done(((f32[4,2,128,128]{3,2,1,0:T(8,128)}), f32[4,2,128,128]{3,2,1,0:T(8,128)}) %all-reduce.2.cloned.1.call-update) | async-done | bytes 524304 | tf_op jit(solution)/shard_map/psum | solution.py:42
  65.3 1.2 %constant_dynamic-slice_fusion = f32[4,2,128,32]{3,2,1,0:T(8,128)S(1)} fusion(f32[4,2,128,128]{3,2,1,0:T(8,128)} %all-reduce.2.cloned.1.call-done, s32[]{:T(128)S(6)} %select_n.8), kind=kLoop, calls=%fused_computation.125 | loop fusion | bytes 262148 | tf_op jit(solution)/shard_map/dynamic_slice | solution.py:45
  66.6 0.8 copy.77
  67.4 3.4 %all-to-all-start = ((f32[2,2,2,32,128]{4,2,1,0,3:T(2,128)}), f32[2,2,2,32,128]{4,2,1,0,3:T(2,128)S(1)}, u32[]{:S(2)}, u32[]{:S(2)}) async-start(f32[2,2,2,32,128]{4,2,1,0,3:T(2,128)} %copy.77), calls=%async_computation | async-start | bytes 262144 | tf_op jit(solution)/shard_map/all_to_all | solution.py:18
  70.8 0.1 broadcast_compare_fusion
  70.9 4.4 %all-to-all-done = f32[2,2,2,32,128]{4,2,1,0,3:T(2,128)S(1)} async-done(((f32[2,2,2,32,128]{4,2,1,0,3:T(2,128)}), f32[2,2,2,32,128]{4,2,1,0,3:T(2,128)S(1)}, u32[]{:S(2)}, u32[]{:S(2)}) %all-to-all-start) | async-done | bytes 131104 | tf_op jit(solution)/shard_map/all_to_all | solution.py:18
  75.3 0.7 copy.79
  75.9 4.6 %all-to-all-start.1 = ((f32[4,2,2,16,128]{4,3,2,1,0:T(8,128)}), f32[4,2,2,16,128]{4,3,2,1,0:T(8,128)}, u32[]{:S(2)}, u32[]{:S(2)}) async-start(f32[4,2,2,16,128]{4,3,2,1,0:T(8,128)} %bitcast.54), calls=%async_computation.1 | async-start | bytes 262144 | tf_op jit(solution)/shard_map/all_to_all | solution.py:17
  80.5 0.1 iota_compare_fusion
  80.6 6.0 %all-to-all-done.1 = f32[4,2,2,16,128]{4,3,2,1,0:T(8,128)} async-done(((f32[4,2,2,16,128]{4,3,2,1,0:T(8,128)}), f32[4,2,2,16,128]{4,3,2,1,0:T(8,128)}, u32[]{:S(2)}, u32[]{:S(2)}) %all-to-all-start.1) | async-done | bytes 131104 | tf_op jit(solution)/shard_map/all_to_all | solution.py:17
  86.6 3.4 %all-to-all-start.2 = ((f32[4,2,2,16,128]{4,3,2,1,0:T(8,128)}), f32[4,2,2,16,128]{4,3,2,1,0:T(8,128)S(1)}, u32[]{:S(2)}, u32[]{:S(2)}) async-start(f32[4,2,2,16,128]{4,3,2,1,0:T(8,128)} %all-to-all-done.1), calls=%async_computation.2 | async-start | bytes 262144 | tf_op jit(solution)/shard_map/all_to_all | solution.py:24
  90.0 0.0 copy-done.4
  90.0 0.1 copy.60
  90.1 4.3 %all-to-all-done.2 = f32[4,2,2,16,128]{4,3,2,1,0:T(8,128)S(1)} async-done(((f32[4,2,2,16,128]{4,3,2,1,0:T(8,128)}), f32[4,2,2,16,128]{4,3,2,1,0:T(8,128)S(1)}, u32[]{:S(2)}, u32[]{:S(2)}) %all-to-all-start.2) | async-done | bytes 131104 | tf_op jit(solution)/shard_map/all_to_all | solution.py:24
  94.4 1.7 %fusion.192 = f32[4,2,32,128]{3,2,1,0:T(8,128)} fusion(f32[2,2,2,32,128]{4,3,2,1,0:T(8,128)S(1)} %copy.81, f32[4,2,128,128]{3,2,1,0:T(8,128)} %all-reduce.2.cloned.1.call-done, s32[]{:T(128)S(6)} %select_n.8, pred[4,2]{1,0:T(4,128)(4,1)S(1)} %copy.60, pred[4,2,128]{2,1,0:T(4,128)(4,1)S(1)} %iota_compare_fusion, pred[4,2,32]{2,1,0:T(4,128)(4,1)S(1)} %broadcast_compare_fusion), kind=kLoop, calls=%fused_computation.65 | loop fusion | flops 131072 | bytes 394508 | tf_op jit(solution)/shard_map/jit(_where)/select_n | solution.py:54
  (5 shorter events, 0.1 us)
Async XLA Ops:
  6.5 6.7 %copy-start = (bf16[1,1,64,128,128]{4,3,2,1,0:T(8,128)(2,1)S(1)}, bf16[1,1,64,128,128]{4,3,2,1,0:T(8,128)(2,1)}, u32[]{:S(2)}) copy-start(bf16[1,1,64,128,128]{4,3,2,1,0:T(8,128)(2,1)} %param.5) | copy-start | bytes 6291460
  6.5 58.8 %all-reduce.2.cloned.1.call-start = ((), (), s32[]{:S(2)}) async-start(), calls=%async_computation.3 | async-start | bytes 1048576 | tf_op jit(solution)/shard_map/psum | solution.py:42
  13.2 2.6 %copy-start.2 = (bf16[4,2,128,128]{3,2,1,0:T(8,128)(2,1)S(1)}, bf16[4,2,128,128]{3,2,1,0:T(8,128)(2,1)}, u32[]{:S(2)}) copy-start(bf16[4,2,128,128]{3,2,1,0:T(8,128)(2,1)} %param.4) | copy-start | bytes 786436
  26.7 2.6 %copy-start.3 = (s32[4,2]{0,1:T(2,128)S(1)}, s32[4,2]{0,1:T(2,128)}, u32[]{:S(2)}) copy-start(s32[4,2]{0,1:T(2,128)} %param.6) | copy-start | bytes 100
  28.5 0.8 copy-start.1
  28.5 61.5 %copy-start.4 = (s32[4,2]{0,1:T(2,128)S(1)}, s32[4,2]{0,1:T(2,128)}, u32[]{:S(2)}) copy-start(s32[4,2]{0,1:T(2,128)} %param.7) | copy-start | bytes 100
  67.4 7.8 %all-to-all-start = ((f32[2,2,2,32,128]{4,2,1,0,3:T(2,128)}), f32[2,2,2,32,128]{4,2,1,0,3:T(2,128)S(1)}, u32[]{:S(2)}, u32[]{:S(2)}) async-start(f32[2,2,2,32,128]{4,2,1,0,3:T(2,128)} %copy.77), calls=%async_computation | async-start | bytes 262144 | tf_op jit(solution)/shard_map/all_to_all | solution.py:18
  75.9 10.6 %all-to-all-start.1 = ((f32[4,2,2,16,128]{4,3,2,1,0:T(8,128)}), f32[4,2,2,16,128]{4,3,2,1,0:T(8,128)}, u32[]{:S(2)}, u32[]{:S(2)}) async-start(f32[4,2,2,16,128]{4,3,2,1,0:T(8,128)} %bitcast.54), calls=%async_computation.1 | async-start | bytes 262144 | tf_op jit(solution)/shard_map/all_to_all | solution.py:17
  86.6 7.8 %all-to-all-start.2 = ((f32[4,2,2,16,128]{4,3,2,1,0:T(8,128)}), f32[4,2,2,16,128]{4,3,2,1,0:T(8,128)S(1)}, u32[]{:S(2)}, u32[]{:S(2)}) async-start(f32[4,2,2,16,128]{4,3,2,1,0:T(8,128)} %all-to-all-done.1), calls=%async_computation.2 | async-start | bytes 262144 | tf_op jit(solution)/shard_map/all_to_all | solution.py:24
Sparse Core Ops, SparseCore 0:
  29.4 35.8 all-reduce.1
where the time goes:
time: 104 us; the launch traced here: 103 us
  waiting for transfers between devices  50.6 us (49%)
  matrix products  15.1 us (15%)
  between operations  13.6 us (13%)
  starting transfers between devices  11.4 us (11%)
  other arithmetic  6.83 us (7%)
  local copies, waits for them, and re-layouts  5.45 us (5%)
    psum x1, waiting for transfers between devices, on_device(): ladder_sum = lax.psum(partials, 'vc')  35.9 us
    dot_general x8, matrix products, ladder_tile(): jnp.einsum('qad,qbd->ab', half_tile, domain, preferred_element_type=jnp.f...  15.1 us
    all_to_all x1, waiting for transfers between devices, mirrored_pairs(): lax.all_to_all(lax.all_to_all(sectioned, 'row', split_axis=3, concat_axis...  5.95 us
    convert_element_type x8, other arithmetic, on_device(): inside = (positions < pno_counts[row_slot, col_slot]).astype(jnp.bfloat16)  4.98 us
    all_to_all x1, starting transfers between devices, mirrored_pairs(): lax.all_to_all(lax.all_to_all(sectioned, 'row', split_axis=3, concat_axis...  4.6 us
    all_to_all x1, waiting for transfers between devices, mirrored_pairs(): lax.all_to_all(sectioned, 'row', split_axis=3, concat_axis=0, tiled=True)  4.38 us
    all_to_all x1, waiting for transfers between devices, mirrored_pairs(): lax.all_to_all(arrived, 'row', split_axis=0, concat_axis=3, tiled=True)  4.33 us
    all_to_all x1, starting transfers between devices, mirrored_pairs(): lax.all_to_all(sectioned, 'row', split_axis=3, concat_axis=0, tiled=True)  3.38 us
  transfers between devices with their start and end apart: 4, of which 4 were waited for; matrix products, arithmetic and copies ran while one was open for 0% of the time, Pallas kernels for 0%

commit v1 on v0

v1 whole, which is shorter than its diff:
```python
import functools
import math

import jax
import jax.numpy as jnp
from jax import lax
from jax.experimental import pallas as pl
from jax.experimental.pallas import tpu as pltpu
from jax.sharding import PartitionSpec as P

AXES = ("row", "col", "vc")
CORES = 2
Q_BLOCK = 16
ROWS_LAST = (((1,), (1,)), ((), ()))


def add_blocks(first, last, domain, masked, total, half_a, half_b, loaded=None):
    virtuals = domain.shape[1]
    pairs = total.shape[0] // virtuals

    def contract(block, half):
        slab = domain[pl.ds(block * Q_BLOCK, Q_BLOCK)]
        stacked = slab.reshape(Q_BLOCK * virtuals, virtuals)
        for group in range(0, pairs, 2):
            product = jnp.dot(
                stacked,
                masked[:, group * virtuals : (group + 2) * virtuals],
                preferred_element_type=jnp.float32,
            ).astype(jnp.bfloat16)
            for pair in (group, group + 1):
                lane = (pair - group) * virtuals
                for q in range(Q_BLOCK):
                    half[
                        pair * virtuals : (pair + 1) * virtuals, q * virtuals : (q + 1) * virtuals
                    ] = product[q * virtuals : (q + 1) * virtuals, lane : lane + virtuals]

    def accumulate(block, half):
        slab = domain[pl.ds(block * Q_BLOCK, Q_BLOCK)]
        beside = jnp.concatenate([slab[q] for q in range(Q_BLOCK)], axis=1)
        total[...] += lax.dot_general(
            half[...], beside, ROWS_LAST, preferred_element_type=jnp.float32
        )

    buffers = (half_a, half_b)
    peeled = 1
    for i in range(peeled):
        if loaded is not None:
            loaded(first + i)
        contract(first + i, buffers[i % 2])
        if i > 0:
            accumulate(first + i - 1, buffers[(i - 1) % 2])
    if loaded is not None:
        for block in range(first + peeled, last):
            loaded(block)
    done, filled = first + peeled - 1, (peeled - 1) % 2
    held, spare = buffers[filled], buffers[1 - filled]

    @pl.loop(0, (last - 1 - done) // 2)
    def _(i):
        contract(done + 2 * i + 1, spare)
        accumulate(done + 2 * i, held)
        contract(done + 2 * i + 2, held)
        accumulate(done + 2 * i + 1, spare)

    if (last - 1 - done) % 2:
        contract(last - 1, spare)
        accumulate(last - 2, held)
        accumulate(last - 1, spare)
    else:
        accumulate(last - 1, held)


def split_rows(total, flipped, slabs, outs):
    virtuals = total.shape[1]
    pairs = total.shape[0] // virtuals
    per_side = math.isqrt(pairs)
    slab_rows, chips = virtuals // slabs, slabs // CORES
    vc_index = lax.axis_index("vc")
    core, chip = lax.rem(vc_index, CORES), vc_index // CORES
    for pair in range(pairs):
        at = slice(pair * virtuals, (pair + 1) * virtuals)
        flipped[at, :] = total[at, :].T
    for (core_step, chip_step, kind), out in outs.items():
        to_core = core if core_step == 0 else 1 - core
        start = (lax.rem(chip + chip_step, chips) * CORES + to_core) * slab_rows
        for pair in range(pairs):
            at = pl.ds(pl.multiple_of(pair * virtuals + start, slab_rows), slab_rows)
            if kind == 0:
                out[pair] = total[at, :]
            else:
                out[pair % per_side * per_side + pair // per_side] = flipped[at, :]


def places_of(core_step, array):
    return {
        (core_step, t, kind): array.at[t, kind] for t in range(array.shape[0]) for kind in range(2)
    }


def first_kernel(
    counts_in, amps_in, domain_in, keep, give, domain, masked_next,
    counts, amps, masked, total, flipped, half_a, half_b, small_sems, domain_sems,
):
    aux, virtuals = domain.shape[:2]
    per_side, row_slots = counts.shape
    halves = row_slots // per_side
    col_index = lax.axis_index("col")

    def domain_copy(block):
        rows = pl.ds(block * Q_BLOCK, Q_BLOCK)
        return pltpu.make_async_copy(domain_in.at[rows], domain.at[rows], domain_sems.at[block])

    def amps_copy(k):
        rows = pl.ds(lax.rem(col_index + k, halves) * per_side, per_side)
        return pltpu.make_async_copy(amps_in.at[rows], amps.at[k], small_sems.at[k])

    def mask(k, out):
        rows = lax.broadcasted_iota(jnp.int32, (virtuals, virtuals), 0)
        cols = lax.broadcasted_iota(jnp.int32, (virtuals, virtuals), 1)
        reach = jnp.maximum(rows, cols)
        half_index = lax.rem(col_index + k, halves)
        for pair in range(per_side * per_side):
            row_slot, col_slot = pair // per_side, pair % per_side
            tile = amps[k, row_slot, col_slot].astype(jnp.float32)
            limit = counts[col_slot, half_index * per_side + row_slot]
            kept = jnp.where(reach < limit, tile, 0.0)
            out[:, pair * virtuals : (pair + 1) * virtuals] = kept.astype(jnp.bfloat16)

    counts_copy = pltpu.make_async_copy(counts_in, counts, small_sems.at[halves])
    counts_copy.start()
    amps_copy(0).start()
    amps_copy(1).start()
    for block in range(aux // Q_BLOCK):
        domain_copy(block).start()
    total[...] = jnp.zeros_like(total)
    counts_copy.wait()
    amps_copy(0).wait()
    mask(0, masked)
    amps_copy(1).wait()
    mask(1, masked_next)
    add_blocks(
        0, aux // Q_BLOCK, domain, masked, total, half_a, half_b,
        lambda block: domain_copy(block).wait(),
    )
    split_rows(
        total, flipped, keep.shape[0] * CORES, {**places_of(0, keep), **places_of(1, give)}
    )


def opening_kernel(last, masked, domain, total, half_a, half_b):
    total[...] = jnp.zeros_like(total)
    add_blocks(0, last, domain, masked, total, half_a, half_b)


def closing_kernel(
    first, masked, total_in, domain, keep, give, give_first, total, flipped, half_a, half_b
):
    chips = keep.shape[0]
    total[...] = total_in[...]
    blocks = domain.shape[0] // Q_BLOCK
    add_blocks(first, blocks, domain, masked, total, half_a, half_b)
    outs = places_of(0, keep)
    for t in range(chips):
        outs[1, t, 0] = give.at[t]
    outs[1, 0, 1] = give.at[chips]
    for t in range(1, chips):
        outs[1, t, 1] = give_first.at[t - 1]
    split_rows(total, flipped, chips * CORES, outs)


def ladder_calls(slabs, counts, amps, domain):
    aux, virtuals = domain.shape[:2]
    per_side, row_slots = counts.shape
    pairs = per_side * per_side
    chips = slabs // CORES

    def rows_of(*ahead):
        return jax.ShapeDtypeStruct((*ahead, pairs, virtuals // slabs, virtuals), jnp.float32)

    made = rows_of(chips, 2)
    masked = jax.ShapeDtypeStruct((virtuals, pairs * virtuals), jnp.bfloat16)
    total = jax.ShapeDtypeStruct((pairs * virtuals, virtuals), jnp.float32)
    half = jax.ShapeDtypeStruct((pairs * virtuals, Q_BLOCK * virtuals), jnp.bfloat16)
    vmem = pl.BlockSpec(memory_space=pltpu.VMEM)
    hbm = pl.BlockSpec(memory_space=pltpu.HBM)

    def call(kernel, name, span, in_specs, outs, scratch, more_scratch=()):
        return pl.pallas_call(
            kernel,
            in_specs=in_specs,
            out_specs=[vmem] * len(outs),
            out_shape=outs,
            scratch_shapes=[pltpu.VMEM(x.shape, x.dtype) for x in scratch] + list(more_scratch),
            compiler_params=pltpu.CompilerParams(vmem_limit_bytes=32 * 2**20),
            cost_estimate=pl.CostEstimate(
                flops=4 * pairs * span * Q_BLOCK * virtuals**3,
                bytes_accessed=2 * span * Q_BLOCK * virtuals**2,
                transcendentals=0,
            ),
            name=name,
        )

    def first_half():
        operands = [pltpu.with_memory_space_constraint(x, pltpu.HBM) for x in (counts, amps, domain)]

        def kernel(*refs):
            *arrays, counts_here, small_sems, domain_sems = refs
            first_kernel(*arrays[:7], counts_here, *arrays[7:], small_sems, domain_sems)

        return call(
            kernel,
            "first_half",
            aux // Q_BLOCK,
            [hbm] * 3,
            [made, made, jax.ShapeDtypeStruct(domain.shape, domain.dtype), masked],
            [
                jax.ShapeDtypeStruct((row_slots // per_side, per_side, *amps.shape[1:]), amps.dtype),
                masked, total, total, half, half,
            ],
            [
                pltpu.SMEM(counts.shape, counts.dtype),
                pltpu.SemaphoreType.DMA((row_slots // per_side + 1,)),
                pltpu.SemaphoreType.DMA((aux // Q_BLOCK,)),
            ],
        )(*operands)

    def second_opens(last, masked_1, domain):
        return call(
            functools.partial(opening_kernel, last), "second_opens", last, [vmem] * 2, [total], [half, half]
        )(masked_1, domain)[0]

    def second_closes(first, masked_1, total_1, domain):
        return call(
            functools.partial(closing_kernel, first),
            "second_closes",
            aux // Q_BLOCK - first,
            [vmem] * 3,
            [made, rows_of(chips + 1), rows_of(chips - 1)],
            [total, total, half, half],
        )(masked_1, total_1, domain)

    return first_half, second_opens, second_closes


def on_device(rows, cols, slabs, amplitudes, factors, pno_counts, pair_live):
    row_slots, per_side = amplitudes.shape[:2]
    halves = row_slots // per_side
    slab_rows, virtuals = amplitudes.shape[2] // slabs, amplitudes.shape[2]
    domain = factors[0, 0]
    row_index, col_index, vc_index = (lax.axis_index(name) for name in AXES)
    reach = jnp.maximum(
        vc_index * slab_rows + lax.broadcasted_iota(jnp.int32, (slab_rows, virtuals), 0),
        lax.broadcasted_iota(jnp.int32, (slab_rows, virtuals), 1),
    )
    limits = jnp.where(pair_live > 0, pno_counts, 0)
    kept_cells = lax.optimization_barrier(
        (reach[None, None] < limits[:, :, None, None]).astype(jnp.float32)
    )

    def send(array, target):
        places = [(r, c, v) for r in range(rows) for c in range(cols) for v in range(slabs)]

        def flat(r, c, v):
            return (r * cols + c) * slabs + v

        return lax.ppermute(array, AXES, [(flat(*place), flat(*target(*place))) for place in places])

    def to_chips(given):
        return [
            send(part, lambda r, c, v, t=t: (r, c, (v + t * CORES) % slabs))
            for t, part in enumerate(given, 1)
        ]

    def mirror_of(k, r, c):
        return c // halves, r * halves + (c + k) % halves

    def to_mirror(k, flipped):
        def target(r, c, v):
            return (r, c, v ^ 1) if mirror_of(k, r, c) == (r, c) else (*mirror_of(k, r, c), v)

        got = send(flipped, target)
        if not any(mirror_of(k, r, c) == (r, c) for r in range(rows) for c in range(cols)):
            return got
        at_row, at_col = mirror_of(k, row_index, col_index)
        return jnp.where((at_row == row_index) & (at_col == col_index), flipped, got)

    def sum_of(*parts):
        return functools.reduce(jnp.add, parts)

    tie = lax.optimization_barrier
    opening, chips = 1, slabs // CORES
    assert halves == 2
    first_half, second_opens, second_closes = ladder_calls(slabs, pno_counts.T, amplitudes, domain)

    def to_core(give):
        return send(give, lambda r, c, v: (r, c, v ^ 1))

    keep_0, give_0, domain, masked_1 = first_half()
    got_0 = to_core(give_0)
    opened = second_opens(opening, masked_1, domain)
    got_0, opened = tie((got_0, opened))
    parts_0 = to_chips([keep_0[t] + got_0[t] for t in range(1, chips)])
    keep_1, give_1, give_first = second_closes(opening, masked_1, opened, domain)
    give_1, give_first, parts_0 = tie((give_1, give_first, parts_0))
    flipped_0 = sum_of(keep_0[0, 1], got_0[0, 1], *[part[1] for part in parts_0])
    mirror_0 = to_mirror(0, flipped_0)
    got_first = to_core(give_first)
    given = [keep_1[t, 1] + got_first[t - 1] for t in range(1, chips)]
    flips = to_chips(given)
    got_1 = to_core(tie((give_1, given))[0])
    flipped_1 = sum_of(keep_1[0, 1], got_1[chips], *flips)
    given = [keep_1[t, 0] + got_1[t] for t in range(1, chips)]
    flipped_1, given = tie((flipped_1, given))
    mirror_1 = to_mirror(1, flipped_1)
    owns = to_chips(given)
    done = [
        sum_of(keep_0[0, 0], got_0[0, 0], *[part[0] for part in parts_0], mirror_0),
        sum_of(keep_1[0, 0], got_1[0], mirror_1, *owns),
    ]
    done = [x.reshape(per_side, per_side, slab_rows, virtuals) for x in done]
    turn = lax.rem(col_index, halves)
    ordered = []
    for half in range(halves):
        value = done[half]
        for other in range(1, halves):
            value = jnp.where(turn == other, done[(half - other) % halves], value)
        ordered.append(value)
    return jnp.where(kept_cells > 0, jnp.concatenate(ordered), 0.0)


def solution(mesh):
    in_specs = (
        P("row", "col", None, None),
        P("row", "col", "vc", None, None),
        P("row", "col"),
        P("row", "col"),
    )
    body = functools.partial(on_device, *(mesh.shape[name] for name in AXES))
    return jax.shard_map(
        body, mesh=mesh, in_specs=in_specs, out_specs=P("row", "col", "vc", None), check_vma=False
    )
```

time: 104 us -> 29.5 us (0.28)
  the two profiles are of different devices: /device:TPU:0 before, /device:TPU:4 now
where the time goes in v1:
time: 29.5 us; the launch traced here: 29.2 us
  Pallas kernels  13 us (44%)
  starting transfers between devices  11 us (37%)
  waiting for transfers between devices  4.11 us (14%)
  other arithmetic  0.95 us (3%)
    ppermute x8, starting transfers between devices, send(): lax.ppermute(array, AXES, [(flat(*place), flat(*target(*place))) for plac...  11 us
    pallas_call x1, Pallas kernels, first_half(): call(kernel, 'first_half', aux // Q_BLOCK, [hbm] * 3, [made, made, jax.Sh...  7.48 us
    pallas_call x1, Pallas kernels, second_closes(): call(functools.partial(closing_kernel, first), 'second_closes', aux // Q_...  4.18 us
    ppermute x8, waiting for transfers between devices, send(): lax.ppermute(array, AXES, [(flat(*place), flat(*target(*place))) for plac...  4.11 us
    pallas_call x1, Pallas kernels, second_opens(): call(functools.partial(opening_kernel, last), 'second_opens', last, [vmem...  1.32 us
    select_n x1, other arithmetic, on_device(): return jnp.where(kept_cells > 0, jnp.concatenate(ordered), 0.0)  0.67 us
  transfers between devices with their start and end apart: 8, of which 7 were waited for; matrix products, arithmetic and copies ran while one was open for 1% of the time, Pallas kernels for 19%

profile of v1, /device:TPU:4, one launch (start us, length us, event | category | flops | bytes accessed | tf_op | source)
XLA Modules:
  0.0 29.2 jit_solution(4088848728696143688)
XLA Ops:
  0.0 7.5 %first_half.1 = (f32[2,2,4,32,128]{4,3,2,1,0:T(8,128)S(1)}, f32[2,2,4,32,128]{4,3,2,1,0:T(8,128)S(1)}, bf16[64,128,128]{2,1,0:T(8,128)(2,1)S(1)}, bf16[128,512]{1,0:T(8,128)(2,1)S(1)}) custom-call(s32[2,4]{1,0:T(2,128)} %bitcast.50, bf16[4,2,128,128]{3,2,1,0:T(8,128)(2,1)} %refs_1_.1, bf16[64,128,128]{2,1,0:T(8,128)(2,1)} %bitcast.51), custom_call_target="tpu_custom_call" | custom-call | flops 2147483648 | bytes 2097152 | tf_op jit(solution)/shard_map/first_half/pallas_call | solution.py:210
  7.5 0.1 collective-permute-start
  7.6 1.3 %second_opens.1.total_in = f32[512,128]{1,0:T(8,128)S(1)} custom-call(bf16[128,512]{1,0:T(8,128)(2,1)S(1)} %get-tuple-element.20.masked, bf16[64,128,128]{2,1,0:T(8,128)(2,1)S(1)} %get-tuple-element.22.domain), custom_call_target="tpu_custom_call" | custom-call | flops 536870912 | bytes 524288 | tf_op jit(solution)/shard_map/second_opens/pallas_call | solution.py:228
  8.9 0.1 iota_maximum_fusion
  9.0 0.1 collective-permute-done
  9.1 0.0 copy-start
  9.1 0.0 copy-start.1
  9.1 1.6 %collective-permute-start.1 = (f32[2,4,32,128]{3,2,1,0:T(8,128)S(1)}, f32[2,4,32,128]{3,2,1,0:T(8,128)S(1)}, u32[]{:S(2)}, u32[]{:S(2)}) collective-permute-start(f32[2,4,32,128]{3,2,1,0:T(8,128)S(1)} %add_bitcast_fusion), channel_id=1, source_target_pairs={{0,2},{1,3},{2,0},{3,1},{4,6},{5,7},{6,4},{7,5},{8,10},{9,11},{10,... | collective-permute-start | bytes 393224 | tf_op jit(solution)/shard_map/ppermute | solution.py:266
  10.7 4.2 %second_closes.1 = (f32[2,2,4,32,128]{4,3,2,1,0:T(8,128)S(1)}, f32[3,4,32,128]{3,2,1,0:T(8,128)S(1)}, f32[1,4,32,128]{3,2,1,0:T(8,128)S(1)}) custom-call(bf16[128,512]{1,0:T(8,128)(2,1)S(1)} %get-tuple-element.20.masked, f32[512,128]{1,0:T(8,128)S(1)} %second_opens.1.total_in, bf16[64,128,128]{2,1,0:T(8,128)(2,1)S(1)} %get-tuple-element.22.domain), custom_call_target="tpu_custom_call" | custom-call | flops 1610612736 | bytes 1572864 | tf_op jit(solution)/shard_map/second_closes/pallas_call | solution.py:233
  14.9 0.1 collective-permute-done.1
  15.0 0.1 collective-permute-start.2
  15.1 0.0 copy-done
  15.1 0.0 copy-done.1
  15.1 0.1 copy.5
  15.2 1.1 %collective-permute-done.2 = f32[1,4,32,128]{3,2,1,0:T(8,128)S(1)} collective-permute-done((f32[1,4,32,128]{3,2,1,0:T(8,128)S(1)}, f32[1,4,32,128]{3,2,1,0:T(8,128)S(1)}, u32[]{:S(2)}, u32[]{:S(2)}) %collective-permute-start.2) | collective-permute-done | bytes 65568 | tf_op jit(solution)/shard_map/ppermute | solution.py:266
  16.2 1.6 %collective-permute-start.4 = (f32[4,32,128]{2,1,0:T(8,128)S(1)}, f32[4,32,128]{2,1,0:T(8,128)S(1)}, u32[]{:S(2)}, u32[]{:S(2)}) collective-permute-start(f32[4,32,128]{2,1,0:T(8,128)S(1)} %bitcast_add_fusion.2), channel_id=1, source_target_pairs={{0,2},{1,3},{2,0},{3,1},{4,6},{5,7},{6,4},{7,5},{8,10},{9,11},{10,... | collective-permute-start | bytes 196616 | tf_op jit(solution)/shard_map/ppermute | solution.py:266
  17.8 0.0 collective-permute-start.3
  17.8 2.6 %collective-permute-start.7 = (f32[4,32,128]{2,1,0:T(8,128)S(1)}, f32[4,32,128]{2,1,0:T(8,128)S(1)}, u32[]{:S(2)}, u32[]{:S(2)}) collective-permute-start(f32[4,32,128]{2,1,0:T(8,128)S(1)} %bitcast_add_fusion), channel_id=1, source_target_pairs={{0,1},{1,0},{2,3},{3,2},{4,5},{5,4},{6,7},{7,6},{8,16},{9,17},{10,... | collective-permute-start | bytes 196616 | tf_op jit(solution)/shard_map/ppermute | solution.py:266
  20.4 0.2 collective-permute-done.4
  20.6 0.0 collective-permute-done.3
  20.6 3.6 %collective-permute-start.5 = (f32[4,32,128]{2,1,0:T(8,128)S(1)}, f32[4,32,128]{2,1,0:T(8,128)S(1)}, u32[]{:S(2)}, u32[]{:S(2)}) collective-permute-start(f32[4,32,128]{2,1,0:T(8,128)S(1)} %get-tuple-element.32), channel_id=1, source_target_pairs={{0,4},{1,5},{2,6},{3,7},{4,0},{5,1},{6,2},{7,3},{8,20},{9,21},{10,... | collective-permute-start | bytes 196616 | tf_op jit(solution)/shard_map/ppermute | solution.py:266
  24.2 1.5 %collective-permute-start.6 = (f32[4,32,128]{2,1,0:T(8,128)S(1)}, f32[4,32,128]{2,1,0:T(8,128)S(1)}, u32[]{:S(2)}, u32[]{:S(2)}) collective-permute-start(f32[4,32,128]{2,1,0:T(8,128)S(1)} %get-tuple-element.33), channel_id=1, source_target_pairs={{0,2},{1,3},{2,0},{3,1},{4,6},{5,7},{6,4},{7,5},{8,10},{9,11},{10,... | collective-permute-start | bytes 196616 | tf_op jit(solution)/shard_map/ppermute | solution.py:266
  25.7 0.1 compare_convert_fusion
  25.8 0.1 collective-permute-done.7
  25.9 1.7 %collective-permute-done.5 = f32[4,32,128]{2,1,0:T(8,128)S(1)} collective-permute-done((f32[4,32,128]{2,1,0:T(8,128)S(1)}, f32[4,32,128]{2,1,0:T(8,128)S(1)}, u32[]{:S(2)}, u32[]{:S(2)}) %collective-permute-start.5) | collective-permute-done | bytes 65568 | tf_op jit(solution)/shard_map/ppermute | solution.py:266
  27.6 0.8 %collective-permute-done.6 = f32[4,32,128]{2,1,0:T(8,128)S(1)} collective-permute-done((f32[4,32,128]{2,1,0:T(8,128)S(1)}, f32[4,32,128]{2,1,0:T(8,128)S(1)}, u32[]{:S(2)}, u32[]{:S(2)}) %collective-permute-start.6) | collective-permute-done | bytes 65568 | tf_op jit(solution)/shard_map/ppermute | solution.py:266
  28.5 0.7 %maximum_select_fusion = f32[4,2,32,128]{3,2,1,0:T(8,128)} fusion(f32[2,2,32,128]{3,2,1,0:T(8,128)S(1)} %bitcast.49, f32[2,2,32,128]{3,2,1,0:T(8,128)S(1)} %bitcast.48, f32[4,2,32,128]{3,2,1,0:T(8,128)S(1)} %compare_convert_fusion), kind=kLoop, calls=%fused_computation | loop fusion | flops 98304 | bytes 393216 | tf_op jit(solution)/shard_map/jit(_where)/select_n | solution.py:328
  (8 shorter events, 0.1 us)
Async XLA Ops:
  7.5 1.6 %collective-permute-start = (f32[2,2,4,32,128]{4,3,2,1,0:T(8,128)S(1)}, f32[2,2,4,32,128]{4,3,2,1,0:T(8,128)S(1)}, u32[]{:S(2)}, u32[]{:S(2)}) collective-permute-start(f32[2,2,4,32,128]{4,3,2,1,0:T(8,128)S(1)} %get-tuple-element.21), channel_id=1, source_target_pairs={{0,1},{1,0},{2,3},{3,2},{4,5},{5,4},{6,7},{7,6},{8,9},{9,8},{10,11... | collective-permute-start | bytes 786440 | tf_op jit(solution)/shard_map/ppermute | solution.py:266
  9.1 5.9 %copy-start = (s32[4,2]{0,1:T(2,128)S(1)}, s32[4,2]{0,1:T(2,128)}, u32[]{:S(2)}) copy-start(s32[4,2]{0,1:T(2,128)} %param.6) | copy-start | bytes 100
  9.1 5.9 %copy-start.1 = (s32[4,2]{0,1:T(2,128)S(1)}, s32[4,2]{0,1:T(2,128)}, u32[]{:S(2)}) copy-start(s32[4,2]{0,1:T(2,128)} %param.7) | copy-start | bytes 100
  9.1 5.8 %collective-permute-start.1 = (f32[2,4,32,128]{3,2,1,0:T(8,128)S(1)}, f32[2,4,32,128]{3,2,1,0:T(8,128)S(1)}, u32[]{:S(2)}, u32[]{:S(2)}) collective-permute-start(f32[2,4,32,128]{3,2,1,0:T(8,128)S(1)} %add_bitcast_fusion), channel_id=1, source_target_pairs={{0,2},{1,3},{2,0},{3,1},{4,6},{5,7},{6,4},{7,5},{8,10},{9,11},{10,... | collective-permute-start | bytes 393224 | tf_op jit(solution)/shard_map/ppermute | solution.py:266
  15.0 1.3 %collective-permute-start.2 = (f32[1,4,32,128]{3,2,1,0:T(8,128)S(1)}, f32[1,4,32,128]{3,2,1,0:T(8,128)S(1)}, u32[]{:S(2)}, u32[]{:S(2)}) collective-permute-start(f32[1,4,32,128]{3,2,1,0:T(8,128)S(1)} %get-tuple-element.30), channel_id=1, source_target_pairs={{0,1},{1,0},{2,3},{3,2},{4,5},{5,4},{6,7},{7,6},{8,9},{9,8},{10,11... | collective-permute-start | bytes 196616 | tf_op jit(solution)/shard_map/ppermute | solution.py:266
  16.2 4.3 %collective-permute-start.4 = (f32[4,32,128]{2,1,0:T(8,128)S(1)}, f32[4,32,128]{2,1,0:T(8,128)S(1)}, u32[]{:S(2)}, u32[]{:S(2)}) collective-permute-start(f32[4,32,128]{2,1,0:T(8,128)S(1)} %bitcast_add_fusion.2), channel_id=1, source_target_pairs={{0,2},{1,3},{2,0},{3,1},{4,6},{5,7},{6,4},{7,5},{8,10},{9,11},{10,... | collective-permute-start | bytes 196616 | tf_op jit(solution)/shard_map/ppermute | solution.py:266
  17.8 2.8 %collective-permute-start.3 = (f32[3,4,32,128]{3,2,1,0:T(8,128)S(1)}, f32[3,4,32,128]{3,2,1,0:T(8,128)S(1)}, u32[]{:S(2)}, u32[]{:S(2)}) collective-permute-start(f32[3,4,32,128]{3,2,1,0:T(8,128)S(1)} %get-tuple-element.31), channel_id=1, source_target_pairs={{0,1},{1,0},{2,3},{3,2},{4,5},{5,4},{6,7},{7,6},{8,9},{9,8},{10,11... | collective-permute-start | bytes 589832 | tf_op jit(solution)/shard_map/ppermute | solution.py:266
  17.8 8.1 %collective-permute-start.7 = (f32[4,32,128]{2,1,0:T(8,128)S(1)}, f32[4,32,128]{2,1,0:T(8,128)S(1)}, u32[]{:S(2)}, u32[]{:S(2)}) collective-permute-start(f32[4,32,128]{2,1,0:T(8,128)S(1)} %bitcast_add_fusion), channel_id=1, source_target_pairs={{0,1},{1,0},{2,3},{3,2},{4,5},{5,4},{6,7},{7,6},{8,16},{9,17},{10,... | collective-permute-start | bytes 196616 | tf_op jit(solution)/shard_map/ppermute | solution.py:266
  20.6 7.0 %collective-permute-start.5 = (f32[4,32,128]{2,1,0:T(8,128)S(1)}, f32[4,32,128]{2,1,0:T(8,128)S(1)}, u32[]{:S(2)}, u32[]{:S(2)}) collective-permute-start(f32[4,32,128]{2,1,0:T(8,128)S(1)} %get-tuple-element.32), channel_id=1, source_target_pairs={{0,4},{1,5},{2,6},{3,7},{4,0},{5,1},{6,2},{7,3},{8,20},{9,21},{10,... | collective-permute-start | bytes 196616 | tf_op jit(solution)/shard_map/ppermute | solution.py:266
  24.2 4.3 %collective-permute-start.6 = (f32[4,32,128]{2,1,0:T(8,128)S(1)}, f32[4,32,128]{2,1,0:T(8,128)S(1)}, u32[]{:S(2)}, u32[]{:S(2)}) collective-permute-start(f32[4,32,128]{2,1,0:T(8,128)S(1)} %get-tuple-element.33), channel_id=1, source_target_pairs={{0,2},{1,3},{2,0},{3,1},{4,6},{5,7},{6,4},{7,5},{8,10},{9,11},{10,... | collective-permute-start | bytes 196616 | tf_op jit(solution)/shard_map/ppermute | solution.py:266

commit v2 on v1

--- a/solution.py
+++ b/solution.py
@@ -1,5 +1,4 @@
 import functools
-import math
 
 import jax
 import jax.numpy as jnp
@@ -10,70 +9,83 @@
 
 AXES = ("row", "col", "vc")
 CORES = 2
-Q_BLOCK = 16
+Q_BLOCK = 8
 ROWS_LAST = (((1,), (1,)), ((), ()))
 
 
-def add_blocks(first, last, domain, masked, total, half_a, half_b, loaded=None):
+def add_blocks(first, last, domain, masked, total, half_a, half_b, rows=None, loaded=None, unroll=False):
     virtuals = domain.shape[1]
     pairs = total.shape[0] // virtuals
+    size = half_a.shape[1] // virtuals
+    rows = rows or (virtuals,) * (pairs // 2)
+    places, end = [], 0
+    for pair in range(pairs):
+        places.append((pair, end, rows[pair // 2]))
+        end += rows[pair // 2]
 
     def contract(block, half):
-        slab = domain[pl.ds(block * Q_BLOCK, Q_BLOCK)]
-        stacked = slab.reshape(Q_BLOCK * virtuals, virtuals)
-        for group in range(0, pairs, 2):
+        for group, height in enumerate(rows):
+            if height == 0:
+                continue
+            stacked = domain[pl.ds(block * size, size), :height].reshape(size * height, virtuals)
             product = jnp.dot(
                 stacked,
-                masked[:, group * virtuals : (group + 2) * virtuals],
+                masked[:, 2 * group * virtuals : 2 * (group + 1) * virtuals],
                 preferred_element_type=jnp.float32,
             ).astype(jnp.bfloat16)
-            for pair in (group, group + 1):
-                lane = (pair - group) * virtuals
-                for q in range(Q_BLOCK):
-                    half[
-                        pair * virtuals : (pair + 1) * virtuals, q * virtuals : (q + 1) * virtuals
-                    ] = product[q * virtuals : (q + 1) * virtuals, lane : lane + virtuals]
+            for pair, start, _ in places[2 * group : 2 * (group + 1)]:
+                lane = (pair - 2 * group) * virtuals
+                for q in range(size):
+                    half[start : start + height, q * virtuals : (q + 1) * virtuals] = product[
+                        q * height : (q + 1) * height, lane : lane + virtuals
+                    ]
 
     def accumulate(block, half):
-        slab = domain[pl.ds(block * Q_BLOCK, Q_BLOCK)]
-        beside = jnp.concatenate([slab[q] for q in range(Q_BLOCK)], axis=1)
-        total[...] += lax.dot_general(
-            half[...], beside, ROWS_LAST, preferred_element_type=jnp.float32
+        slab = domain[pl.ds(block * size, size)]
+        beside = jnp.concatenate([slab[q] for q in range(size)], axis=1)
+        added = lax.dot_general(
+            half[:end], beside, ROWS_LAST, preferred_element_type=jnp.float32
         )
-
-    buffers = (half_a, half_b)
-    peeled = 1
-    for i in range(peeled):
-        if loaded is not None:
-            loaded(first + i)
-        contract(first + i, buffers[i % 2])
-        if i > 0:
-            accumulate(first + i - 1, buffers[(i - 1) % 2])
-    if loaded is not None:
-        for block in range(first + peeled, last):
-            loaded(block)
-    done, filled = first + peeled - 1, (peeled - 1) % 2
-    held, spare = buffers[filled], buffers[1 - filled]
-
-    @pl.loop(0, (last - 1 - done) // 2)
+        for pair, start, height in places:
+            if height > 0:
+                total[pair * virtuals : pair * virtuals + height] += added[start : start + height]
+
+    loaded = loaded or (lambda block: None)
+    contract(first, half_a)
+
+    @pl.loop(0, (last - 1 - first) // 2, unroll=unroll)
     def _(i):
-        contract(done + 2 * i + 1, spare)
-        accumulate(done + 2 * i, held)
-        contract(done + 2 * i + 2, held)
-        accumulate(done + 2 * i + 1, spare)
-
-    if (last - 1 - done) % 2:
-        contract(last - 1, spare)
-        accumulate(last - 2, held)
-        accumulate(last - 1, spare)
+        loaded(first + 2 * i + 1)
+        loaded(first + 2 * i + 2)
+        contract(first + 2 * i + 1, half_b)
+        accumulate(first + 2 * i, half_a)
+        contract(first + 2 * i + 2, half_a)
+        accumulate(first + 2 * i + 1, half_b)
+
+    if (last - 1 - first) % 2:
+        loaded(last - 1)
+        contract(last - 1, half_b)
+        accumulate(last - 2, half_a)
+        accumulate(last - 1, half_b)
     else:
-        accumulate(last - 1, held)
-
-
-def split_rows(total, flipped, slabs, outs):
+        accumulate(last - 1, half_a)
+
+
+def sides_of(pair, pairs):
+    bits = (pairs.bit_length() - 1) // 2
+    return pair >> bits, pair & ((1 << bits) - 1)
+
+
+def mirror_place(pair, pairs):
+    row, col = sides_of(pair, pairs)
+    return (col << ((pairs.bit_length() - 1) // 2)) | row
+
+
+def split_rows(total, flipped, slabs, outs, order=None):
     virtuals = total.shape[1]
     pairs = total.shape[0] // virtuals
-    per_side = math.isqrt(pairs)
+    order = order or range(pairs)
+    mirrors = [mirror_place(pair, pairs) for pair in order]
     slab_rows, chips = virtuals // slabs, slabs // CORES
     vc_index = lax.axis_index("vc")
     core, chip = lax.rem(vc_index, CORES), vc_index // CORES
@@ -83,12 +95,12 @@
     for (core_step, chip_step, kind), out in outs.items():
         to_core = core if core_step == 0 else 1 - core
         start = (lax.rem(chip + chip_step, chips) * CORES + to_core) * slab_rows
-        for pair in range(pairs):
-            at = pl.ds(pl.multiple_of(pair * virtuals + start, slab_rows), slab_rows)
+        for tile, (pair, mirror) in enumerate(zip(order, mirrors)):
+            at = pl.ds(pl.multiple_of(tile * virtuals + start, slab_rows), slab_rows)
             if kind == 0:
                 out[pair] = total[at, :]
             else:
-                out[pair % per_side * per_side + pair // per_side] = flipped[at, :]
+                out[mirror] = flipped[at, :]
 
 
 def places_of(core_step, array):
@@ -98,12 +110,14 @@
 
 
 def first_kernel(
-    counts_in, amps_in, domain_in, keep, give, domain, masked_next,
-    counts, amps, masked, total, flipped, half_a, half_b, small_sems, domain_sems,
+    counts_in, live_in, amps_in, domain_in, keep, give, domain, masked_next,
+    counts, live, amps, masked, total, flipped, half_a, half_b, small_sems, domain_sems,
 ):
     aux, virtuals = domain.shape[:2]
     per_side, row_slots = counts.shape
+    pairs = per_side * per_side
     halves = row_slots // per_side
+    blocks = aux // Q_BLOCK
     col_index = lax.axis_index("col")
 
     def domain_copy(block):
@@ -114,42 +128,64 @@
         rows = pl.ds(lax.rem(col_index + k, halves) * per_side, per_side)
         return pltpu.make_async_copy(amps_in.at[rows], amps.at[k], small_sems.at[k])
 
-    def mask(k, out):
+    def limit(k, pair):
+        slot = lax.rem(col_index + k, halves) * per_side + pair // per_side
+        return jnp.where(live[pair % per_side, slot] > 0, counts[pair % per_side, slot], 0)
+
+    def mask(k, out, limits, order):
         rows = lax.broadcasted_iota(jnp.int32, (virtuals, virtuals), 0)
         cols = lax.broadcasted_iota(jnp.int32, (virtuals, virtuals), 1)
         reach = jnp.maximum(rows, cols)
-        half_index = lax.rem(col_index + k, halves)
-        for pair in range(per_side * per_side):
-            row_slot, col_slot = pair // per_side, pair % per_side
-            tile = amps[k, row_slot, col_slot].astype(jnp.float32)
-            limit = counts[col_slot, half_index * per_side + row_slot]
-            kept = jnp.where(reach < limit, tile, 0.0)
-            out[:, pair * virtuals : (pair + 1) * virtuals] = kept.astype(jnp.bfloat16)
-
-    counts_copy = pltpu.make_async_copy(counts_in, counts, small_sems.at[halves])
-    counts_copy.start()
-    amps_copy(0).start()
-    amps_copy(1).start()
-    for block in range(aux // Q_BLOCK):
+        for tile, pair in enumerate(order):
+            amp = amps[k, *sides_of(pair, pairs)].astype(jnp.float32)
+            kept = jnp.where(reach < limits[tile], amp, 0.0)
+            out[:, tile * virtuals : (tile + 1) * virtuals] = kept.astype(jnp.bfloat16)
+
+    copies = [
+        pltpu.make_async_copy(counts_in, counts, small_sems.at[halves]),
+        pltpu.make_async_copy(live_in, live, small_sems.at[halves + 1]),
+        *[amps_copy(k) for k in range(halves)],
+    ]
+    for copy in copies:
+        copy.start()
+    for block in range(blocks):
         domain_copy(block).start()
     total[...] = jnp.zeros_like(total)
-    counts_copy.wait()
-    amps_copy(0).wait()
-    mask(0, masked)
-    amps_copy(1).wait()
-    mask(1, masked_next)
-    add_blocks(
-        0, aux // Q_BLOCK, domain, masked, total, half_a, half_b,
-        lambda block: domain_copy(block).wait(),
-    )
+    for copy in copies:
+        copy.wait()
+    keys = [limit(0, pair) * pairs + pair for pair in range(pairs)]
+    for done in range(pairs - 1):
+        for i in range(pairs - 1 - done):
+            keys[i : i + 2] = jnp.maximum(*keys[i : i + 2]), jnp.minimum(*keys[i : i + 2])
+    limits = [key >> (pairs.bit_length() - 1) for key in keys]
+    order = [key & (pairs - 1) for key in keys]
+    mask(0, masked, limits, order)
+    mask(1, masked_next, [limit(1, pair) for pair in range(pairs)], range(pairs))
+    domain_copy(0).wait()
+
+    levels = [0, virtuals // 2, 3 * virtuals // 4, virtuals]
+    reached = [sum((x > bound).astype(jnp.int32) for bound in levels[:-1]) for x in limits[::2]]
+    for high in range(len(levels)):
+        for low in range(high + 1):
+            @pl.when((reached[0] == high) & (reached[1] == low))
+            def _(rows=(levels[high], levels[low])):
+                if rows[0] == 0:
+                    for block in range(1, blocks):
+                        domain_copy(block).wait()
+                else:
+                    add_blocks(
+                        0, blocks, domain, masked, total, half_a, half_b, rows,
+                        lambda block: domain_copy(block).wait(),
+                    )
+
     split_rows(
-        total, flipped, keep.shape[0] * CORES, {**places_of(0, keep), **places_of(1, give)}
-    )
-
-
-def opening_kernel(last, masked, domain, total, half_a, half_b):
+        total, flipped, keep.shape[0] * CORES, {**places_of(0, keep), **places_of(1, give)}, order
+    )
+
+
+def opening_kernel(masked, domain, total, half):
     total[...] = jnp.zeros_like(total)
-    add_blocks(0, last, domain, masked, total, half_a, half_b)
+    add_blocks(0, 1, domain, masked, total, half, half)
 
 
 def closing_kernel(
@@ -158,7 +194,7 @@
     chips = keep.shape[0]
     total[...] = total_in[...]
     blocks = domain.shape[0] // Q_BLOCK
-    add_blocks(first, blocks, domain, masked, total, half_a, half_b)
+    add_blocks(first, blocks, domain, masked, total, half_a, half_b, unroll=True)
     outs = places_of(0, keep)
     for t in range(chips):
         outs[1, t, 0] = give.at[t]
@@ -168,7 +204,7 @@
     split_rows(total, flipped, chips * CORES, outs)
 
 
-def ladder_calls(slabs, counts, amps, domain):
+def ladder_calls(slabs, counts, live, amps, domain):
     aux, virtuals = domain.shape[:2]
     per_side, row_slots = counts.shape
     pairs = per_side * per_side
@@ -180,7 +216,11 @@
     made = rows_of(chips, 2)
     masked = jax.ShapeDtypeStruct((virtuals, pairs * virtuals), jnp.bfloat16)
     total = jax.ShapeDtypeStruct((pairs * virtuals, virtuals), jnp.float32)
-    half = jax.ShapeDtypeStruct((pairs * virtuals, Q_BLOCK * virtuals), jnp.bfloat16)
+
+    def half_of(size):
+        return jax.ShapeDtypeStruct((pairs * virtuals, size * virtuals), jnp.bfloat16)
+
+    half = half_of(Q_BLOCK)
     vmem = pl.BlockSpec(memory_space=pltpu.VMEM)
     hbm = pl.BlockSpec(memory_space=pltpu.HBM)
 
@@ -201,17 +241,17 @@
         )
 
     def first_half():
-        operands = [pltpu.with_memory_space_constraint(x, pltpu.HBM) for x in (counts, amps, domain)]
+        operands = [pltpu.with_memory_space_constraint(x, pltpu.HBM) for x in (counts, live, amps, domain)]
 
         def kernel(*refs):
-            *arrays, counts_here, small_sems, domain_sems = refs
-            first_kernel(*arrays[:7], counts_here, *arrays[7:], small_sems, domain_sems)
+            *arrays, counts_here, live_here, small_sems, domain_sems = refs
+            first_kernel(*arrays[:8], counts_here, live_here, *arrays[8:], small_sems, domain_sems)
 
         return call(
             kernel,
             "first_half",
             aux // Q_BLOCK,
-            [hbm] * 3,
+            [hbm] * 4,
             [made, made, jax.ShapeDtypeStruct(domain.shape, domain.dtype), masked],
             [
                 jax.ShapeDtypeStruct((row_slots // per_side, per_side, *amps.shape[1:]), amps.dtype),
@@ -219,14 +259,15 @@
             ],
             [
                 pltpu.SMEM(counts.shape, counts.dtype),
-                pltpu.SemaphoreType.DMA((row_slots // per_side + 1,)),
+                pltpu.SMEM(live.shape, live.dtype),
+                pltpu.SemaphoreType.DMA((row_slots // per_side + 2,)),
                 pltpu.SemaphoreType.DMA((aux // Q_BLOCK,)),
             ],
         )(*operands)
 
     def second_opens(last, masked_1, domain):
         return call(
-            functools.partial(opening_kernel, last), "second_opens", last, [vmem] * 2, [total], [half, half]
+            opening_kernel, "second_opens", last, [vmem] * 2, [total], [half_of(last * Q_BLOCK)]
         )(masked_1, domain)[0]
 
     def second_closes(first, masked_1, total_1, domain):
@@ -288,9 +329,9 @@
         return functools.reduce(jnp.add, parts)
 
     tie = lax.optimization_barrier
-    opening, chips = 1, slabs // CORES
+    opening, chips = 2, slabs // CORES
     assert halves == 2
-    first_half, second_opens, second_closes = ladder_calls(slabs, pno_counts.T, amplitudes, domain)
+    first_half, second_opens, second_closes = ladder_calls(slabs, pno_counts.T, pair_live.T, amplitudes, domain)
 
     def to_core(give):
         return send(give, lambda r, c, v: (r, c, v ^ 1))

time: 29.5 us -> 28.2 us (0.956); the launches traced: 29.2 us -> 28.6 us
  Pallas kernels: 13 us -> 11.5 us
  starting transfers between devices: 11 us -> 11.5 us
    pallas_call x2, Pallas kernels: 8.79 us -> 7.6 us  [the longest x1 6.29 us: first_half(): call(kernel, 'first_half', aux // Q_BLOCK, [hbm] * 4, [made, made, jax.Sh...]
    ppermute x8, starting transfers between devices: 11 us -> 11.5 us  [send(): lax.ppermute(array, AXES, [(flat(*place), flat(*target(*place))) for plac...]
  transfers between devices with their start and end apart: 8 -> 8, of which waited for: 7 -> 6; matrix products, arithmetic and copies ran while one was open for 1% -> 1% of each run, Pallas kernels for 19% -> 18%
where the time goes in v2:
time: 28.2 us; the launch traced here: 28.6 us
  Pallas kernels  11.5 us (41%)
  starting transfers between devices  11.5 us (41%)
  waiting for transfers between devices  4.38 us (16%)
  other arithmetic  0.95 us (3%)
    ppermute x8, starting transfers between devices, send(): lax.ppermute(array, AXES, [(flat(*place), flat(*target(*place))) for plac...  11.5 us
    pallas_call x1, Pallas kernels, first_half(): call(kernel, 'first_half', aux // Q_BLOCK, [hbm] * 4, [made, made, jax.Sh...  6.29 us
    ppermute x8, waiting for transfers between devices, send(): lax.ppermute(array, AXES, [(flat(*place), flat(*target(*place))) for plac...  4.38 us
    pallas_call x1, Pallas kernels, second_closes(): call(functools.partial(closing_kernel, first), 'second_closes', aux // Q_...  3.94 us
    pallas_call x1, Pallas kernels, second_opens(): call(opening_kernel, 'second_opens', last, [vmem] * 2, [total], [half_of(...  1.32 us
    select_n x1, other arithmetic, on_device(): return jnp.where(kept_cells > 0, jnp.concatenate(ordered), 0.0)  0.67 us
  transfers between devices with their start and end apart: 8, of which 6 were waited for; matrix products, arithmetic and copies ran while one was open for 1% of the time, Pallas kernels for 18%

profile of v2, /device:TPU:4, one launch (start us, length us, event | category | flops | bytes accessed | tf_op | source)
XLA Modules:
  0.0 28.6 jit_solution(9846684569833988478)
XLA Ops:
  0.0 6.3 %first_half.1 = (f32[2,2,4,32,128]{4,3,2,1,0:T(8,128)S(1)}, f32[2,2,4,32,128]{4,3,2,1,0:T(8,128)S(1)}, bf16[64,128,128]{2,1,0:T(8,128)(2,1)S(1)}, bf16[128,512]{1,0:T(8,128)(2,1)S(1)}) custom-call(s32[2,4]{1,0:T(2,128)} %bitcast.51, s32[2,4]{1,0:T(2,128)} %bitcast.52, bf16[4,2,128,128]{3,2,1,0:T(8,128)(2,1)} %refs_2_.1, bf16[64,128,128]{2,1,0:T(8,128)(2,1)} %bitcast.53), custom_call_target="tpu_custom_call" | custom-call | flops 2147483648 | bytes 2097152 | tf_op jit(solution)/shard_map/first_half/pallas_call | solution.py:250
  6.3 0.1 collective-permute-start
  6.4 1.3 %second_opens.1.total_in = f32[512,128]{1,0:T(8,128)S(1)} custom-call(bf16[128,512]{1,0:T(8,128)(2,1)S(1)} %get-tuple-element.20.masked, bf16[64,128,128]{2,1,0:T(8,128)(2,1)S(1)} %get-tuple-element.22.domain), custom_call_target="tpu_custom_call" | custom-call | flops 536870912 | bytes 524288 | tf_op jit(solution)/shard_map/second_opens/pallas_call | solution.py:269
  7.7 0.1 iota_maximum_fusion
  7.8 0.1 collective-permute-done
  7.9 0.0 copy-start
  7.9 0.0 copy-start.1
  7.9 1.6 %collective-permute-start.1 = (f32[2,4,32,128]{3,2,1,0:T(8,128)S(1)}, f32[2,4,32,128]{3,2,1,0:T(8,128)S(1)}, u32[]{:S(2)}, u32[]{:S(2)}) collective-permute-start(f32[2,4,32,128]{3,2,1,0:T(8,128)S(1)} %add_bitcast_fusion), channel_id=1, source_target_pairs={{0,2},{1,3},{2,0},{3,1},{4,6},{5,7},{6,4},{7,5},{8,10},{9,11},{10,... | collective-permute-start | bytes 393224 | tf_op jit(solution)/shard_map/ppermute | solution.py:307
  9.5 3.9 %second_closes.1 = (f32[2,2,4,32,128]{4,3,2,1,0:T(8,128)S(1)}, f32[3,4,32,128]{3,2,1,0:T(8,128)S(1)}, f32[1,4,32,128]{3,2,1,0:T(8,128)S(1)}) custom-call(bf16[128,512]{1,0:T(8,128)(2,1)S(1)} %get-tuple-element.20.masked, f32[512,128]{1,0:T(8,128)S(1)} %second_opens.1.total_in, bf16[64,128,128]{2,1,0:T(8,128)(2,1)S(1)} %get-tuple-element.22.domain), custom_call_target="tpu_custom_call" | custom-call | flops 1610612736 | bytes 1572864 | tf_op jit(solution)/shard_map/second_closes/pallas_call | solution.py:274
  13.5 0.3 %collective-permute-done.1 = f32[2,4,32,128]{3,2,1,0:T(8,128)S(1)} collective-permute-done((f32[2,4,32,128]{3,2,1,0:T(8,128)S(1)}, f32[2,4,32,128]{3,2,1,0:T(8,128)S(1)}, u32[]{:S(2)}, u32[]{:S(2)}) %collective-permute-start.1) | collective-permute-done | bytes 131104 | tf_op jit(solution)/shard_map/ppermute | solution.py:307
  13.8 0.0 collective-permute-start.2
  13.8 0.0 copy-done
  13.8 0.0 copy-done.1
  13.8 0.1 copy.5
  13.9 1.1 %collective-permute-done.2 = f32[1,4,32,128]{3,2,1,0:T(8,128)S(1)} collective-permute-done((f32[1,4,32,128]{3,2,1,0:T(8,128)S(1)}, f32[1,4,32,128]{3,2,1,0:T(8,128)S(1)}, u32[]{:S(2)}, u32[]{:S(2)}) %collective-permute-start.2) | collective-permute-done | bytes 65568 | tf_op jit(solution)/shard_map/ppermute | solution.py:307
  15.1 1.6 %collective-permute-start.4 = (f32[4,32,128]{2,1,0:T(8,128)S(1)}, f32[4,32,128]{2,1,0:T(8,128)S(1)}, u32[]{:S(2)}, u32[]{:S(2)}) collective-permute-start(f32[4,32,128]{2,1,0:T(8,128)S(1)} %bitcast_add_fusion.2), channel_id=1, source_target_pairs={{0,2},{1,3},{2,0},{3,1},{4,6},{5,7},{6,4},{7,5},{8,10},{9,11},{10,... | collective-permute-start | bytes 196616 | tf_op jit(solution)/shard_map/ppermute | solution.py:307
  16.6 0.0 collective-permute-start.3
  16.6 2.6 %collective-permute-start.7 = (f32[4,32,128]{2,1,0:T(8,128)S(1)}, f32[4,32,128]{2,1,0:T(8,128)S(1)}, u32[]{:S(2)}, u32[]{:S(2)}) collective-permute-start(f32[4,32,128]{2,1,0:T(8,128)S(1)} %bitcast_add_fusion), channel_id=1, source_target_pairs={{0,1},{1,0},{2,3},{3,2},{4,5},{5,4},{6,7},{7,6},{8,16},{9,17},{10,... | collective-permute-start | bytes 196616 | tf_op jit(solution)/shard_map/ppermute | solution.py:307
  19.2 0.2 collective-permute-done.4
  19.4 0.0 collective-permute-done.3
  19.4 4.2 %collective-permute-start.5 = (f32[4,32,128]{2,1,0:T(8,128)S(1)}, f32[4,32,128]{2,1,0:T(8,128)S(1)}, u32[]{:S(2)}, u32[]{:S(2)}) collective-permute-start(f32[4,32,128]{2,1,0:T(8,128)S(1)} %get-tuple-element.32), channel_id=1, source_target_pairs={{0,4},{1,5},{2,6},{3,7},{4,0},{5,1},{6,2},{7,3},{8,20},{9,21},{10,... | collective-permute-start | bytes 196616 | tf_op jit(solution)/shard_map/ppermute | solution.py:307
  23.6 1.5 %collective-permute-start.6 = (f32[4,32,128]{2,1,0:T(8,128)S(1)}, f32[4,32,128]{2,1,0:T(8,128)S(1)}, u32[]{:S(2)}, u32[]{:S(2)}) collective-permute-start(f32[4,32,128]{2,1,0:T(8,128)S(1)} %get-tuple-element.33), channel_id=1, source_target_pairs={{0,2},{1,3},{2,0},{3,1},{4,6},{5,7},{6,4},{7,5},{8,10},{9,11},{10,... | collective-permute-start | bytes 196616 | tf_op jit(solution)/shard_map/ppermute | solution.py:307
  25.1 0.1 compare_convert_fusion
  25.2 0.0 collective-permute-done.7
  25.2 1.3 %collective-permute-done.5 = f32[4,32,128]{2,1,0:T(8,128)S(1)} collective-permute-done((f32[4,32,128]{2,1,0:T(8,128)S(1)}, f32[4,32,128]{2,1,0:T(8,128)S(1)}, u32[]{:S(2)}, u32[]{:S(2)}) %collective-permute-start.5) | collective-permute-done | bytes 65568 | tf_op jit(solution)/shard_map/ppermute | solution.py:307
  26.5 1.4 %collective-permute-done.6 = f32[4,32,128]{2,1,0:T(8,128)S(1)} collective-permute-done((f32[4,32,128]{2,1,0:T(8,128)S(1)}, f32[4,32,128]{2,1,0:T(8,128)S(1)}, u32[]{:S(2)}, u32[]{:S(2)}) %collective-permute-start.6) | collective-permute-done | bytes 65568 | tf_op jit(solution)/shard_map/ppermute | solution.py:307
  27.9 0.7 %maximum_select_fusion = f32[4,2,32,128]{3,2,1,0:T(8,128)} fusion(f32[2,2,32,128]{3,2,1,0:T(8,128)S(1)} %bitcast.50, f32[2,2,32,128]{3,2,1,0:T(8,128)S(1)} %bitcast.49, f32[4,2,32,128]{3,2,1,0:T(8,128)S(1)} %compare_convert_fusion), kind=kLoop, calls=%fused_computation | loop fusion | flops 98304 | bytes 393216 | tf_op jit(solution)/shard_map/jit(_where)/select_n | solution.py:369
  (8 shorter events, 0.1 us)
Async XLA Ops:
  6.3 1.6 %collective-permute-start = (f32[2,2,4,32,128]{4,3,2,1,0:T(8,128)S(1)}, f32[2,2,4,32,128]{4,3,2,1,0:T(8,128)S(1)}, u32[]{:S(2)}, u32[]{:S(2)}) collective-permute-start(f32[2,2,4,32,128]{4,3,2,1,0:T(8,128)S(1)} %get-tuple-element.21), channel_id=1, source_target_pairs={{0,1},{1,0},{2,3},{3,2},{4,5},{5,4},{6,7},{7,6},{8,9},{9,8},{10,11... | collective-permute-start | bytes 786440 | tf_op jit(solution)/shard_map/ppermute | solution.py:307
  7.9 5.9 %copy-start = (s32[4,2]{0,1:T(2,128)S(1)}, s32[4,2]{0,1:T(2,128)}, u32[]{:S(2)}) copy-start(s32[4,2]{0,1:T(2,128)} %param.6) | copy-start | bytes 100
  7.9 5.9 %copy-start.1 = (s32[4,2]{0,1:T(2,128)S(1)}, s32[4,2]{0,1:T(2,128)}, u32[]{:S(2)}) copy-start(s32[4,2]{0,1:T(2,128)} %param.7) | copy-start | bytes 100
  7.9 5.8 %collective-permute-start.1 = (f32[2,4,32,128]{3,2,1,0:T(8,128)S(1)}, f32[2,4,32,128]{3,2,1,0:T(8,128)S(1)}, u32[]{:S(2)}, u32[]{:S(2)}) collective-permute-start(f32[2,4,32,128]{3,2,1,0:T(8,128)S(1)} %add_bitcast_fusion), channel_id=1, source_target_pairs={{0,2},{1,3},{2,0},{3,1},{4,6},{5,7},{6,4},{7,5},{8,10},{9,11},{10,... | collective-permute-start | bytes 393224 | tf_op jit(solution)/shard_map/ppermute | solution.py:307
  13.8 1.3 %collective-permute-start.2 = (f32[1,4,32,128]{3,2,1,0:T(8,128)S(1)}, f32[1,4,32,128]{3,2,1,0:T(8,128)S(1)}, u32[]{:S(2)}, u32[]{:S(2)}) collective-permute-start(f32[1,4,32,128]{3,2,1,0:T(8,128)S(1)} %get-tuple-element.30), channel_id=1, source_target_pairs={{0,1},{1,0},{2,3},{3,2},{4,5},{5,4},{6,7},{7,6},{8,9},{9,8},{10,11... | collective-permute-start | bytes 196616 | tf_op jit(solution)/shard_map/ppermute | solution.py:307
  15.1 4.3 %collective-permute-start.4 = (f32[4,32,128]{2,1,0:T(8,128)S(1)}, f32[4,32,128]{2,1,0:T(8,128)S(1)}, u32[]{:S(2)}, u32[]{:S(2)}) collective-permute-start(f32[4,32,128]{2,1,0:T(8,128)S(1)} %bitcast_add_fusion.2), channel_id=1, source_target_pairs={{0,2},{1,3},{2,0},{3,1},{4,6},{5,7},{6,4},{7,5},{8,10},{9,11},{10,... | collective-permute-start | bytes 196616 | tf_op jit(solution)/shard_map/ppermute | solution.py:307
  16.6 2.8 %collective-permute-start.3 = (f32[3,4,32,128]{3,2,1,0:T(8,128)S(1)}, f32[3,4,32,128]{3,2,1,0:T(8,128)S(1)}, u32[]{:S(2)}, u32[]{:S(2)}) collective-permute-start(f32[3,4,32,128]{3,2,1,0:T(8,128)S(1)} %get-tuple-element.31), channel_id=1, source_target_pairs={{0,1},{1,0},{2,3},{3,2},{4,5},{5,4},{6,7},{7,6},{8,9},{9,8},{10,11... | collective-permute-start | bytes 589832 | tf_op jit(solution)/shard_map/ppermute | solution.py:307
  16.6 8.5 %collective-permute-start.7 = (f32[4,32,128]{2,1,0:T(8,128)S(1)}, f32[4,32,128]{2,1,0:T(8,128)S(1)}, u32[]{:S(2)}, u32[]{:S(2)}) collective-permute-start(f32[4,32,128]{2,1,0:T(8,128)S(1)} %bitcast_add_fusion), channel_id=1, source_target_pairs={{0,1},{1,0},{2,3},{3,2},{4,5},{5,4},{6,7},{7,6},{8,16},{9,17},{10,... | collective-permute-start | bytes 196616 | tf_op jit(solution)/shard_map/ppermute | solution.py:307
  19.4 7.0 %collective-permute-start.5 = (f32[4,32,128]{2,1,0:T(8,128)S(1)}, f32[4,32,128]{2,1,0:T(8,128)S(1)}, u32[]{:S(2)}, u32[]{:S(2)}) collective-permute-start(f32[4,32,128]{2,1,0:T(8,128)S(1)} %get-tuple-element.32), channel_id=1, source_target_pairs={{0,4},{1,5},{2,6},{3,7},{4,0},{5,1},{6,2},{7,3},{8,20},{9,21},{10,... | collective-permute-start | bytes 196616 | tf_op jit(solution)/shard_map/ppermute | solution.py:307
  23.6 4.3 %collective-permute-start.6 = (f32[4,32,128]{2,1,0:T(8,128)S(1)}, f32[4,32,128]{2,1,0:T(8,128)S(1)}, u32[]{:S(2)}, u32[]{:S(2)}) collective-permute-start(f32[4,32,128]{2,1,0:T(8,128)S(1)} %get-tuple-element.33), channel_id=1, source_target_pairs={{0,2},{1,3},{2,0},{3,1},{4,6},{5,7},{6,4},{7,5},{8,10},{9,11},{10,... | collective-permute-start | bytes 196616 | tf_op jit(solution)/shard_map/ppermute | solution.py:307
